TPU v7x, 1024 devices: a whole 4x4x32 slice. The times are simulated.
1024 devices in a mesh: gx: 8 (over z_hi, core), gy: 16 (over x, y), gz: 8 (over z_lo).
Axes of the slice: x: 4, y: 4, z: 32 (z_hi: 4, z_lo: 8; z = z_hi * 8 + z_lo), core: 2. Of those that a mesh axis runs over, the one named last changes fastest.
Arguments:
- offsets: float32 [3, 16, 32, 16, 128], P(None, 'gx', 'gy', 'gz'), may hold values from 0 to 1
- velocity: float32 [3, 16, 32, 16, 128], P(None, 'gx', 'gy', 'gz'), may hold values from -6 to 6
- mass: float32 [16, 32, 16, 128], P('gx', 'gy', 'gz'), may hold values from 0.005 to 0.02
- counts: int32 [16, 32, 16], P('gx', 'gy', 'gz'), may hold values from 1 to 128
Outputs:
- accel: float32 [3, 16, 32, 16, 128], P(None, 'gx', 'gy', 'gz')
- density: float32 [16, 32, 16, 128], P('gx', 'gy', 'gz')
Inputs may be any that keep to these rules, and one draw needn't show every extreme that they name: `counts`: slots of a cell at or beyond its count are empty.
All inputs are finite; a program needn't handle non-finite values.
Results may differ from a plain program's by a relative error of at most 0.0003.
Values sent between devices are 32-bit elements; how exact they have to be, the bound alone decides.
A program may use at most 64 MiB of HBM per device.

v0:
```python
import functools
import math

import jax
import jax.numpy as jnp
from jax import lax
from jax.experimental import pallas as pl
from jax.experimental.pallas import tpu as pltpu
from jax.sharding import PartitionSpec as P

KERNEL_NORM = 315.0 / (64.0 * math.pi)
GRADIENT_RATIO = 6.0
PRESSURE_COEF = 0.5
AXES = ("gx", "gy", "gz")
SIDES = (-1, 0, 1)
MESH = pl.DeviceIdType.MESH
F32 = jnp.float32
TILE = 32


def span_own(step):
    if isinstance(step, int):
        return pl.ds(0, 2) if step == 0 else pl.ds((step + 1) // 2, 1)
    return pl.ds((step + 1) // 2, 1)


def span_halo(step):
    if isinstance(step, int):
        return pl.ds(1, 2) if step == 0 else pl.ds(0 if step < 0 else 3, 1)
    return pl.ds(3 * ((step + 1) // 2), 1)


def slot(step):
    return (step[0] + 1) * 9 + (step[1] + 1) * 3 + (step[2] + 1)


def kernel(sizes, off, vel, mass, cnt, acc_out, den_out, own, near, u_own, u_near, own_b, s_b, dens, force, quad,
           send1, recv1, send2, recv2):
    me = tuple(lax.axis_index(a) for a in AXES)
    near_x = 1 - 2 * lax.rem(me[0], 2)
    far_x = -near_x
    plane_dirs = [(0, b, c) for b in SIDES for c in SIDES if (b, c) != (0, 0)]
    near_dirs = [(near_x, b, c) for b in SIDES for c in SIDES]
    far_dirs = [(far_x, b, c) for b in SIDES for c in SIDES]
    all_dirs = far_dirs + near_dirs + plane_dirs

    def other(step):
        return tuple(m + s for m, s in zip(me, step))

    def exists(step):
        ok = None
        for m, s, n in zip(me, step, sizes):
            if isinstance(s, int) and s == 0:
                continue
            here = jnp.logical_and(m + s >= 0, m + s < n)
            ok = here if ok is None else jnp.logical_and(ok, here)
        return ok

    def neg(step):
        return tuple(-s for s in step)

    barrier = pltpu.get_barrier_semaphore()
    for step in all_dirs:
        @pl.when(exists(step))
        def _():
            pl.semaphore_signal(barrier, inc=1, device_id=other(step), device_id_type=MESH)

    lanes = lax.broadcasted_iota(jnp.int32, (1, 128), 1)
    for x in range(2):
        for y in range(2):
            for z in range(2):
                pos = [off[k, x, y, z : z + 1, :] + float(c - 1) for k, c in enumerate((x, y, z))]
                m_eff = jnp.where(lanes < cnt[x, y, z], mass[x, y, z : z + 1, :], 0.0)
                sq = pos[0] * pos[0] + pos[1] * pos[1] + pos[2] * pos[2]
                v = [vel[k, x, y, z : z + 1, :] for k in range(3)]
                tile = jnp.concatenate(pos + [m_eff] + v + [sq], axis=0)
                own[x, y, z] = tile
                scaled = jnp.concatenate([p * -6.0 for p in pos] + [m_eff] + v + [1.0 - sq], axis=0)
                near[1 + x, 1 + y, 1 + z] = scaled

    peers = 1
    for m, n in zip(me, sizes):
        peers = peers * (1 + (m > 0).astype(jnp.int32) + (m < n - 1).astype(jnp.int32))
    pl.semaphore_wait(barrier, peers - 1)

    def copy1(step, incoming):
        there = step if incoming else neg(step)
        return pltpu.make_async_remote_copy(
            src_ref=own.at[tuple(span_own(s) for s in step)],
            dst_ref=near.at[tuple(span_halo(s) for s in there)],
            send_sem=send1.at[slot(step)],
            recv_sem=recv1.at[slot(there)],
            device_id=other(step),
            device_id_type=MESH,
        )

    def copy2(step, incoming):
        there = step if incoming else neg(step)
        return pltpu.make_async_remote_copy(
            src_ref=u_own.at[tuple(span_own(s) for s in step)],
            dst_ref=u_near.at[tuple(span_halo(s) for s in there)],
            send_sem=send2.at[slot(step)],
            recv_sem=recv2.at[slot(there)],
            device_id=other(step),
            device_id_type=MESH,
        )

    for step in all_dirs:
        @pl.when(exists(step))
        def _():
            copy1(step, False).start()

    for n in range(8):
        x, y, z = n // 4, (n // 2) % 2, n % 2
        turned = jnp.transpose(own[x, y, z], (1, 0))
        for k in range(3):
            own_b[k, n] = jnp.broadcast_to(turned[:, k : k + 1] * (-1.0 / 3.0), (128, 128))
        own_b[3, n] = jnp.broadcast_to(turned[:, 7:8], (128, 128))

    def cells_own(x, y, z):
        return [(a, b, c) for a in (1, 2) for b in (1, 2) for c in (1, 2)]

    def cells_plane(x, y, z):
        bh, ch = 3 * y, 3 * z
        ring = [(bh, ch), (bh, 1), (bh, 2), (1, ch), (2, ch)]
        return [(a, b, c) for a in (1, 2) for b, c in ring]

    def cells_side(x, y, z):
        return [(3 * x, y + b, z + c) for b in range(3) for c in range(3)]

    def density_tile(n, r0, cells, base, first):
        rows = pl.ds(r0, TILE)
        xi, yi, zi, wi = (own_b[k, n, rows, :] for k in range(4))
        total = jnp.zeros((TILE, 128), F32) if first else dens[n, rows, :]
        for k, (a, b, c) in enumerate(cells):
            t = near[a, b, c]
            q = jnp.maximum(xi * t[0:1] + yi * t[1:2] + zi * t[2:3] + (t[7:8] - wi), 0.0)
            quad[n, base + k, rows, :] = q
            total = total + (q * q) * (q * t[3:4])
        dens[n, rows, :] = total

    def force_tile(n, r0, cells, base, first):
        rows = pl.ds(r0, TILE)
        si = s_b[n, rows, :]
        sums = [jnp.zeros((TILE, 128), F32) if first else force[k, n, rows, :] for k in range(5)]
        for k, (a, b, c) in enumerate(cells):
            t = near[a, b, c]
            q = quad[n, base + k, rows, :]
            q2 = q * q
            pr = q2 * (t[3:4] * si + t[7:8])
            vi = q2 * (q * t[7:8])
            for d in range(3):
                sums[d] = sums[d] + (pr * t[d : d + 1] + vi * t[4 + d : 5 + d])
            sums[3] = sums[3] + pr
            sums[4] = sums[4] + vi
        for k in range(5):
            force[k, n, rows, :] = sums[k]

    def sweep(tile_fn, x_side, cells_of, base, first):
        count = (8 if x_side is None else 4) * (128 // TILE)

        def step(i, carry):
            cell, r0 = i // (128 // TILE), pl.multiple_of((i % (128 // TILE)) * TILE, TILE)
            x = cell // 4 if x_side is None else x_side
            y, z = (cell // 2) % 2, cell % 2
            tile_fn(4 * x + 2 * y + z, r0, cells_of(x, y, z), base, first)
            return carry

        lax.fori_loop(0, count, step, 0)

    def arrive1(dirs):
        for step in dirs:
            region = tuple(span_halo(s) for s in step)

            @pl.when(exists(step))
            def _():
                copy1(step, True).wait_recv()
                t = near[region]
                p = []
                for k in range(3):
                    shift = 2 * step[k]
                    shift = float(shift) if isinstance(shift, int) else shift.astype(F32)
                    p.append(t[:, :, :, k : k + 1, :] + shift)
                sq = p[0] * p[0] + p[1] * p[1] + p[2] * p[2]
                for k in range(3):
                    near[region + (pl.ds(k, 1),)] = p[k] * -6.0
                near[region + (pl.ds(7, 1),)] = 1.0 - sq

            @pl.when(jnp.logical_not(exists(step)))
            def _():
                near[region] = jnp.zeros_like(near[region])

    def arrive2(dirs):
        for step in dirs:
            region = tuple(span_halo(s) for s in step)

            @pl.when(exists(step))
            def _():
                copy2(step, True).wait_recv()
                near[region + (pl.ds(7, 1),)] = u_near[region]

    near_side, far_side = (near_x + 1) // 2, (far_x + 1) // 2
    sweep(density_tile, None, cells_own, 0, True)
    arrive1(plane_dirs)
    sweep(density_tile, None, cells_plane, 8, False)
    arrive1(near_dirs)
    sweep(density_tile, near_side, cells_side, 18, False)
    arrive1(far_dirs)
    sweep(density_tile, far_side, cells_side, 18, False)

    s_rows = []
    for n in range(8):
        x, y, z = n // 4, (n // 2) % 2, n % 2
        rho = KERNEL_NORM * jnp.sum(jnp.transpose(dens[n], (1, 0)), axis=0, keepdims=True)
        held = lanes < cnt[x, y, z]
        rho = jnp.where(held, rho, 0.0)
        den_out[x, y, z : z + 1, :] = rho
        s = PRESSURE_COEF / jnp.where(held, rho, 1.0)
        s_rows.append(s)
        u = own[x, y, z, 3:4, :] * s
        u_own[x, y, z] = u
        near[1 + x, 1 + y, 1 + z, 7:8, :] = u

    for step in all_dirs:
        @pl.when(exists(step))
        def _():
            copy2(step, False).start()

    turned = jnp.transpose(jnp.concatenate(s_rows, axis=0), (1, 0))
    for n in range(8):
        s_b[n] = jnp.broadcast_to(turned[:, n : n + 1], (128, 128))

    sweep(force_tile, None, cells_own, 0, True)
    arrive2(plane_dirs)
    sweep(force_tile, None, cells_plane, 8, False)
    arrive2(near_dirs)
    sweep(force_tile, near_side, cells_side, 18, False)
    arrive2(far_dirs)
    sweep(force_tile, far_side, cells_side, 18, False)

    for n in range(8):
        x, y, z = n // 4, (n // 2) % 2, n % 2
        f = [jnp.sum(jnp.transpose(force[k, n], (1, 0)), axis=0, keepdims=True) for k in range(5)]
        held = lanes < cnt[x, y, z]
        t = own[x, y, z]
        for k in range(3):
            a = KERNEL_NORM * (f[k] + GRADIENT_RATIO * t[k : k + 1] * f[3] - t[4 + k : 5 + k] * f[4])
            acc_out[k, x, y, z : z + 1, :] = jnp.where(held, a, 0.0)

    for step in all_dirs:
        @pl.when(exists(step))
        def _():
            copy1(step, False).wait_send()
            copy2(step, False).wait_send()


def local(sizes, offsets, velocity, mass, counts):
    vmem = pl.BlockSpec(memory_space=pltpu.VMEM)
    return pl.pallas_call(
        functools.partial(kernel, sizes),
        out_shape=(
            jax.ShapeDtypeStruct(offsets.shape, F32),
            jax.ShapeDtypeStruct(mass.shape, F32),
        ),
        in_specs=[vmem, vmem, vmem, pl.BlockSpec(memory_space=pltpu.SMEM)],
        out_specs=(vmem, vmem),
        scratch_shapes=[
            pltpu.VMEM((2, 2, 2, 8, 128), F32),
            pltpu.VMEM((4, 4, 4, 8, 128), F32),
            pltpu.VMEM((2, 2, 2, 1, 128), F32),
            pltpu.VMEM((4, 4, 4, 1, 128), F32),
            pltpu.VMEM((4, 8, 128, 128), F32),
            pltpu.VMEM((8, 128, 128), F32),
            pltpu.VMEM((8, 128, 128), F32),
            pltpu.VMEM((5, 8, 128, 128), F32),
            pltpu.VMEM((8, 27, 128, 128), F32),
            pltpu.SemaphoreType.DMA((27,)),
            pltpu.SemaphoreType.DMA((27,)),
            pltpu.SemaphoreType.DMA((27,)),
            pltpu.SemaphoreType.DMA((27,)),
        ],
        compiler_params=pltpu.CompilerParams(
            collective_id=0, has_side_effects=True, vmem_limit_bytes=40 * 2**20
        ),
        name="sph",
    )(offsets, velocity, mass, counts)


def solution(mesh):
    sizes = tuple(mesh.shape[a] for a in AXES)
    in_specs = (
        P(None, "gx", "gy", "gz", None),
        P(None, "gx", "gy", "gz", None),
        P("gx", "gy", "gz", None),
        P("gx", "gy", "gz"),
    )
    out_specs = (P(None, "gx", "gy", "gz", None), P("gx", "gy", "gz", None))
    return jax.shard_map(
        functools.partial(local, sizes), mesh=mesh, in_specs=in_specs, out_specs=out_specs, check_vma=False
    )
```

profile of v0, /device:TPU:71, one launch (start us, length us, event | category | flops | bytes accessed | tf_op | source)
XLA Modules:
  0.0 54.2 jit_solution(5409412336134257686)
XLA Ops:
  0.6 0.0 copy-start
  0.6 0.7 %copy-done = f32[3,2,2,2,128]{4,3,2,1,0:T(2,128)S(1)} copy-done((f32[3,2,2,2,128]{4,3,2,1,0:T(2,128)S(1)}, f32[3,2,2,2,128]{4,3,2,1,0:T(2,128)}, u32[]{:S(2)}) %copy-start) | copy-done | bytes 12312
  1.3 0.0 copy-start.1
  1.3 0.7 %copy-done.1 = f32[3,2,2,2,128]{4,3,2,1,0:T(2,128)S(1)} copy-done((f32[3,2,2,2,128]{4,3,2,1,0:T(2,128)S(1)}, f32[3,2,2,2,128]{4,3,2,1,0:T(2,128)}, u32[]{:S(2)}) %copy-start.1) | copy-done | bytes 12312
  2.0 0.0 copy-start.2
  2.0 0.7 %copy-done.2 = f32[2,2,2,128]{3,2,1,0:T(2,128)S(1)} copy-done((f32[2,2,2,128]{3,2,1,0:T(2,128)S(1)}, f32[2,2,2,128]{3,2,1,0:T(2,128)}, u32[]{:S(2)}) %copy-start.2) | copy-done | bytes 4120
  2.7 0.0 copy-start.3
  2.7 0.7 %copy-done.3 = s32[2,2,2]{2,1,0:T(2,128)S(1)} copy-done((s32[2,2,2]{2,1,0:T(2,128)S(1)}, s32[2,2,2]{2,1,0:T(2,128)}, u32[]{:S(2)}) %copy-start.3) | copy-done | bytes 56
  3.4 49.5 %sph.1 = (f32[3,2,2,2,128]{4,3,2,1,0:T(2,128)S(1)}, f32[2,2,2,128]{3,2,1,0:T(2,128)S(1)}) custom-call(f32[3,2,2,2,128]{4,3,2,1,0:T(2,128)S(1)} %copy-done, f32[3,2,2,2,128]{4,3,2,1,0:T(2,128)S(1)} %copy-done.1, f32[2,2,2,128]{3,2,1,0:T(2,128)S(1)} %copy-done.2, s32[2,2,2]{2,1,0:T(2,128)S(1)} %copy-done.3), custom_call_target="tpu_custom_call" | custom-call | tf_op jit(solution)/shard_map/sph/pallas_call | solution.py:259
  53.0 0.6 %copy.8 = f32[3,2,2,2,128]{4,3,2,1,0:T(2,128)} copy(f32[3,2,2,2,128]{4,3,2,1,0:T(2,128)S(1)} %get-tuple-element.4) | data formatting | bytes 24576
  53.6 0.6 %copy.9 = f32[2,2,2,128]{3,2,1,0:T(2,128)} copy(f32[2,2,2,128]{3,2,1,0:T(2,128)S(1)} %get-tuple-element.5) | data formatting | bytes 8192
Async XLA Ops:
  0.6 0.7 %copy-start = (f32[3,2,2,2,128]{4,3,2,1,0:T(2,128)S(1)}, f32[3,2,2,2,128]{4,3,2,1,0:T(2,128)}, u32[]{:S(2)}) copy-start(f32[3,2,2,2,128]{4,3,2,1,0:T(2,128)} %off.1) | copy-start | bytes 36868
  1.3 0.7 %copy-start.1 = (f32[3,2,2,2,128]{4,3,2,1,0:T(2,128)S(1)}, f32[3,2,2,2,128]{4,3,2,1,0:T(2,128)}, u32[]{:S(2)}) copy-start(f32[3,2,2,2,128]{4,3,2,1,0:T(2,128)} %vel.1) | copy-start | bytes 36868
  2.0 0.7 %copy-start.2 = (f32[2,2,2,128]{3,2,1,0:T(2,128)S(1)}, f32[2,2,2,128]{3,2,1,0:T(2,128)}, u32[]{:S(2)}) copy-start(f32[2,2,2,128]{3,2,1,0:T(2,128)} %mass.1) | copy-start | bytes 12292
  2.7 0.7 %copy-start.3 = (s32[2,2,2]{2,1,0:T(2,128)S(1)}, s32[2,2,2]{2,1,0:T(2,128)}, u32[]{:S(2)}) copy-start(s32[2,2,2]{2,1,0:T(2,128)} %cnt.1) | copy-start | bytes 100
where the time goes:
time: 54.5 us; the launch traced here: 54.2 us
  Pallas kernels  49.5 us (91%)
  local copies, waits for them, and re-layouts  3.97 us (7%)
  between operations  0.65 us (1%)
    pallas_call x1, Pallas kernels, local(): pl.pallas_call(functools.partial(kernel, sizes), out_shape=(jax.ShapeDtyp...  49.5 us
    unnamed x10, local copies, waits for them, and re-layouts  3.97 us

commit v1 on v0

v1 whole, which is shorter than its diff:
```python
import functools
import math

import jax
import jax.numpy as jnp
from jax import lax
from jax.experimental import pallas as pl
from jax.experimental.pallas import tpu as pltpu
from jax.sharding import PartitionSpec as P

KERNEL_NORM = 315.0 / (64.0 * math.pi)
GRADIENT_RATIO = 6.0
PRESSURE_COEF = 0.5
AXES = ("gx", "gy", "gz")
SIDES = (-1, 0, 1)
MESH = pl.DeviceIdType.MESH
F32 = jnp.float32
BF16 = jnp.bfloat16
TILE = 32
LAST = (((1,), (1,)), ((), ()))
SHARED = (6, 4, 6)


def span_own(step):
    if isinstance(step, int):
        return pl.ds(0, 2) if step == 0 else pl.ds((step + 1) // 2, 1)
    return pl.ds((step + 1) // 2, 1)


def span_halo(step):
    if isinstance(step, int):
        return pl.ds(1, 2) if step == 0 else pl.ds(0 if step < 0 else 3, 1)
    return pl.ds(3 * ((step + 1) // 2), 1)


def slot(step):
    return (step[0] + 1) * 9 + (step[1] + 1) * 3 + (step[2] + 1)


def pieces(x):
    high = x.astype(BF16).astype(F32)
    rest = x - high
    mid = rest.astype(BF16).astype(F32)
    return high, mid, rest - mid


def halves(x):
    high = x.astype(BF16)
    return high, (x - high.astype(F32)).astype(BF16)


def kernel(sizes, off_in, vel_in, mass_in, cnt_in, acc_out, den_out, off, vel, mass, cnt, own, near, u_own, u_near,
           own_q, near_q, near_f, s_b, dens, force, force2, force3, quad, load, send1, recv1, send2, recv2):
    me = tuple(lax.axis_index(a) for a in AXES)
    near_x = 1 - 2 * lax.rem(me[0], 2)
    far_x = -near_x
    plane_dirs = [(0, b, c) for b in SIDES for c in SIDES if (b, c) != (0, 0)]
    near_dirs = [(near_x, b, c) for b in SIDES for c in SIDES]
    far_dirs = [(far_x, b, c) for b in SIDES for c in SIDES]
    all_dirs = far_dirs + near_dirs + plane_dirs

    def other(step):
        return tuple(m + s for m, s in zip(me, step))

    def exists(step):
        ok = None
        for m, s, n in zip(me, step, sizes):
            if isinstance(s, int) and s == 0:
                continue
            here = jnp.logical_and(m + s >= 0, m + s < n)
            ok = here if ok is None else jnp.logical_and(ok, here)
        return ok

    def neg(step):
        return tuple(-s for s in step)

    loads = [
        pltpu.make_async_copy(src, dst, load.at[k])
        for k, (src, dst) in enumerate(((off_in, off), (mass_in, mass), (cnt_in, cnt), (vel_in, vel)))
    ]
    for item in loads:
        item.start()
    barrier = pltpu.get_barrier_semaphore()
    for step in all_dirs:
        @pl.when(exists(step))
        def _():
            pl.semaphore_signal(barrier, inc=1, device_id=other(step), device_id_type=MESH)
    for item in loads:
        item.wait()

    lanes = lax.broadcasted_iota(jnp.int32, (1, 128), 1)
    one = jnp.ones((1, 128), F32)
    blank = jnp.zeros((3, 128), F32)

    def put_near_q(a, b, c, scaled, rest):
        high, mid, low = pieces(jnp.concatenate(scaled + [rest, one, blank], axis=0))
        near_q[a, b, c] = jnp.concatenate([high, mid, high, mid, low, high], axis=0).astype(BF16)

    def own_tile(x, y, z):
        pos = [off[k, x, y, z : z + 1, :] + float(c - 1) for k, c in enumerate((x, y, z))]
        m_eff = jnp.where(lanes < cnt[x, y, z], mass[x, y, z : z + 1, :], 0.0)
        sq = pos[0] * pos[0] + pos[1] * pos[1] + pos[2] * pos[2]
        v = [vel[k, x, y, z : z + 1, :] for k in range(3)]
        return pos, m_eff, v, sq

    for x in range(2):
        for y in range(2):
            for z in range(2):
                pos, m_eff, v, sq = own_tile(x, y, z)
                own[x, y, z] = jnp.concatenate(pos + [m_eff] + v + [sq], axis=0)

    peers = 1
    for m, n in zip(me, sizes):
        peers = peers * (1 + (m > 0).astype(jnp.int32) + (m < n - 1).astype(jnp.int32))
    pl.semaphore_wait(barrier, peers - 1)

    def copy1(step, incoming):
        there = step if incoming else neg(step)
        return pltpu.make_async_remote_copy(
            src_ref=own.at[tuple(span_own(s) for s in step)],
            dst_ref=near.at[tuple(span_halo(s) for s in there)],
            send_sem=send1.at[slot(step)],
            recv_sem=recv1.at[slot(there)],
            device_id=other(step),
            device_id_type=MESH,
        )

    def copy2(step, incoming):
        there = step if incoming else neg(step)
        return pltpu.make_async_remote_copy(
            src_ref=u_own.at[tuple(span_own(s) for s in step)],
            dst_ref=u_near.at[tuple(span_halo(s) for s in there)],
            send_sem=send2.at[slot(step)],
            recv_sem=recv2.at[slot(there)],
            device_id=other(step),
            device_id_type=MESH,
        )

    for step in all_dirs:
        @pl.when(exists(step))
        def _():
            copy1(step, False).start()

    for x in range(2):
        for y in range(2):
            for z in range(2):
                pos, m_eff, v, sq = own_tile(x, y, z)
                scaled = [p * -6.0 for p in pos]
                near[1 + x, 1 + y, 1 + z] = jnp.concatenate(scaled + [m_eff] + v + [jnp.zeros_like(sq)], axis=0)
                put_near_q(1 + x, 1 + y, 1 + z, scaled, 1.0 - sq)
                high, mid, low = pieces(jnp.concatenate([p * (-1.0 / 3.0) for p in pos] + [one, -sq, blank], axis=0))
                stack = jnp.concatenate([high, high, mid, mid, high, low], axis=0)
                own_q[4 * x + 2 * y + z] = jnp.transpose(stack, (1, 0)).astype(BF16)

    def cells_own(x, y, z):
        return [(a, b, c) for a in (1, 2) for b in (1, 2) for c in (1, 2)]

    def cells_plane(x, y, z):
        bh, ch = 3 * y, 3 * z
        shared = [(a, bh, c) for a in (1, 2) for c in (1, 2)]
        return shared + [(a, b, ch) for a in (1, 2) for b in (bh, 1, 2)]

    def cells_side(x, y, z):
        shared = [(3 * x, y + b, c) for b in range(3) for c in (1, 2)]
        return shared + [(3 * x, y + b, 3 * z) for b in range(3)]

    def density_cells(x, cells_of, base, first):
        for y in range(2):
            for z in range(2):
                n = 4 * x + 2 * y + z
                cells = cells_of(x, y, z)
                mine = own_q[n]
                total = jnp.zeros((128, 128), F32) if first else dens[n]
                for k in range(0, len(cells), 2):
                    group = cells[k : k + 2]
                    them = jnp.concatenate([near_q[cell] for cell in group], axis=1)
                    both = jnp.dot(mine, them, preferred_element_type=F32)
                    for i, (a, b, c) in enumerate(group):
                        q = jnp.maximum(both[:, 128 * i : 128 * i + 128], 0.0)
                        quad[n, base + k + i] = q
                        total = total + (q * q) * (q * near[a, b, c, 3:4, :])
                dens[n] = total

    def force_pair(x, y, cells_of, base, shared, first):
        n = 4 * x + 2 * y
        pair = 2 * x + y
        rows2 = jnp.zeros((32, 256), F32) if first else force2[pair]
        rows3 = jnp.zeros((16, 256), F32) if first else force3[pair]
        cells = cells_of(x, y, 0)
        for k in range(0, shared, 2):
            f = jnp.concatenate([near_f[cells[k]], near_f[cells[k + 1]]], axis=1)
            q = jnp.concatenate(
                [jnp.concatenate([quad[n + z, base + k + i] for i in range(2)], axis=1) for z in range(2)], axis=0
            )
            q2 = q * q
            for part in halves(q2):
                rows2 = rows2 + lax.dot_general(f[:32], part, LAST, preferred_element_type=F32)
            for part in halves(q2 * q):
                rows3 = rows3 + lax.dot_general(f[32:], part, LAST, preferred_element_type=F32)
        force2[pair] = rows2
        force3[pair] = rows3
        for z in range(2):
            rest = list(enumerate(cells_of(x, y, z)))[shared:]
            for r0 in range(0, 128, TILE):
                rows = pl.ds(r0, TILE)
                si = s_b[n + z, rows, :]
                sums = [jnp.zeros((TILE, 128), F32) if first else force[k, n + z, rows, :] for k in range(5)]
                for k, (a, b, c) in rest:
                    t = near[a, b, c]
                    q = quad[n + z, base + k, rows, :]
                    q2 = q * q
                    pr = q2 * (t[3:4] * si + t[7:8])
                    vi = q2 * (q * t[7:8])
                    for d in range(3):
                        sums[d] = sums[d] + (pr * t[d : d + 1] + vi * t[4 + d : 5 + d])
                    sums[3] = sums[3] + pr
                    sums[4] = sums[4] + vi
                for k in range(5):
                    force[k, n + z, rows, :] = sums[k]

    def over_x(fn):
        def step(x, carry):
            fn(x)
            return carry

        lax.fori_loop(0, 2, step, 0)

    def force_cells(x, cells_of, base, shared, first):
        for y in range(2):
            force_pair(x, y, cells_of, base, shared, first)

    def corner(step):
        def low(s):
            return 1 if isinstance(s, int) and s == 0 else 3 * ((s + 1) // 2)

        def many(s):
            return 2 if isinstance(s, int) and s == 0 else 1

        return [
            tuple(low(s) + i for s, i in zip(step, (i, j, k)))
            for i in range(many(step[0]))
            for j in range(many(step[1]))
            for k in range(many(step[2]))
        ]

    def arrive1(dirs):
        for step in dirs:
            cells = corner(step)

            @pl.when(exists(step))
            def _():
                copy1(step, True).wait_recv()
                for a, b, c in cells:
                    t = near[a, b, c]
                    pos = []
                    for k in range(3):
                        shift = 2 * step[k]
                        pos.append(t[k : k + 1] + (float(shift) if isinstance(shift, int) else shift.astype(F32)))
                    sq = pos[0] * pos[0] + pos[1] * pos[1] + pos[2] * pos[2]
                    scaled = [p * -6.0 for p in pos]
                    near[a, b, c, 0:3, :] = jnp.concatenate(scaled, axis=0)
                    put_near_q(a, b, c, scaled, 1.0 - sq)

            @pl.when(jnp.logical_not(exists(step)))
            def _():
                for cell in cells:
                    near[cell] = jnp.zeros((8, 128), F32)
                    near_q[cell] = jnp.zeros((48, 128), BF16)

    def put_near_f(a, b, c, u):
        t = near[a, b, c]
        m = t[3:4]
        wide = jnp.concatenate([m] + [m * t[k : k + 1] for k in range(3)] + [u] + [u * t[k : k + 1] for k in range(3)], axis=0)
        thin = jnp.concatenate([u] + [u * t[4 + k : 5 + k] for k in range(3)], axis=0)
        wide3, thin3 = pieces(wide), pieces(thin)
        near_f[a, b, c] = jnp.concatenate(
            list(wide3) + [jnp.zeros_like(wide)] + list(thin3) + [jnp.zeros_like(thin)], axis=0
        ).astype(BF16)

    def arrive2(dirs):
        for step in dirs:
            cells = corner(step)
            inner = isinstance(step[2], int) and step[2] == 0

            @pl.when(exists(step))
            def _():
                copy2(step, True).wait_recv()
                for a, b, c in cells:
                    u = u_near[a, b, c]
                    near[a, b, c, 7:8, :] = u
                    if inner:
                        put_near_f(a, b, c, u)

            if inner:
                @pl.when(jnp.logical_not(exists(step)))
                def _():
                    for cell in cells:
                        near_f[cell] = jnp.zeros((48, 128), BF16)

    near_side, far_side = (near_x + 1) // 2, (far_x + 1) // 2
    over_x(lambda x: density_cells(x, cells_own, 0, True))
    arrive1(plane_dirs)
    over_x(lambda x: density_cells(x, cells_plane, 8, False))
    arrive1(near_dirs)
    density_cells(near_side, cells_side, 18, False)
    arrive1(far_dirs)
    density_cells(far_side, cells_side, 18, False)

    s_rows = []
    for n in range(8):
        x, y, z = n // 4, (n // 2) % 2, n % 2
        rho = KERNEL_NORM * jnp.sum(jnp.transpose(dens[n], (1, 0)), axis=0, keepdims=True)
        held = lanes < cnt[x, y, z]
        rho = jnp.where(held, rho, 0.0)
        den_out[x, y, z : z + 1, :] = rho
        s = PRESSURE_COEF / jnp.where(held, rho, 1.0)
        s_rows.append(s)
        u = own[x, y, z, 3:4, :] * s
        u_own[x, y, z] = u

    for step in all_dirs:
        @pl.when(exists(step))
        def _():
            copy2(step, False).start()

    s_all = jnp.concatenate(s_rows, axis=0)
    turned = jnp.transpose(s_all, (1, 0))
    for n in range(8):
        x, y, z = n // 4, (n // 2) % 2, n % 2
        s_b[n] = jnp.broadcast_to(turned[:, n : n + 1], (128, 128))
        u = own[x, y, z, 3:4, :] * s_rows[n]
        near[1 + x, 1 + y, 1 + z, 7:8, :] = u
        put_near_f(1 + x, 1 + y, 1 + z, u)

    over_x(lambda x: force_cells(x, cells_own, 0, SHARED[0], True))
    arrive2(plane_dirs)
    over_x(lambda x: force_cells(x, cells_plane, 8, SHARED[1], False))
    arrive2(near_dirs)
    force_cells(near_side, cells_side, 18, SHARED[2], False)
    arrive2(far_dirs)
    force_cells(far_side, cells_side, 18, SHARED[2], False)

    for n in range(8):
        x, y, z = n // 4, (n // 2) % 2, n % 2
        f = [jnp.sum(jnp.transpose(force[k, n], (1, 0)), axis=0, keepdims=True) for k in range(5)]
        g = force2[2 * x + y, :, 128 * z : 128 * z + 128]
        g = g[0:8] + g[8:16] + g[16:24]
        h = force3[2 * x + y, :, 128 * z : 128 * z + 128]
        h = h[0:4] + h[4:8] + h[8:12]
        held = lanes < cnt[x, y, z]
        t = own[x, y, z]
        s = s_rows[n]
        press = f[3] + s * g[0:1] + g[4:5]
        drag = f[4] + h[0:1]
        for k in range(3):
            a = f[k] + s * g[1 + k : 2 + k] + g[5 + k : 6 + k] + h[1 + k : 2 + k]
            a = KERNEL_NORM * (a + GRADIENT_RATIO * t[k : k + 1] * press - t[4 + k : 5 + k] * drag)
            acc_out[k, x, y, z : z + 1, :] = jnp.where(held, a, 0.0)

    for step in all_dirs:
        @pl.when(exists(step))
        def _():
            copy1(step, False).wait_send()
            copy2(step, False).wait_send()


def local(sizes, offsets, velocity, mass, counts):
    vmem = pl.BlockSpec(memory_space=pltpu.VMEM)
    hbm = pl.BlockSpec(memory_space=pltpu.HBM)
    return pl.pallas_call(
        functools.partial(kernel, sizes),
        out_shape=(
            jax.ShapeDtypeStruct(offsets.shape, F32),
            jax.ShapeDtypeStruct(mass.shape, F32),
        ),
        in_specs=[hbm, hbm, hbm, hbm],
        out_specs=(vmem, vmem),
        scratch_shapes=[
            pltpu.VMEM(offsets.shape, F32),
            pltpu.VMEM(velocity.shape, F32),
            pltpu.VMEM(mass.shape, F32),
            pltpu.SMEM(counts.shape, jnp.int32),
            pltpu.VMEM((2, 2, 2, 8, 128), F32),
            pltpu.VMEM((4, 4, 4, 8, 128), F32),
            pltpu.VMEM((2, 2, 2, 1, 128), F32),
            pltpu.VMEM((4, 4, 4, 1, 128), F32),
            pltpu.VMEM((8, 128, 48), BF16),
            pltpu.VMEM((4, 4, 4, 48, 128), BF16),
            pltpu.VMEM((4, 4, 4, 48, 128), BF16),
            pltpu.VMEM((8, 128, 128), F32),
            pltpu.VMEM((8, 128, 128), F32),
            pltpu.VMEM((5, 8, 128, 128), F32),
            pltpu.VMEM((4, 32, 256), F32),
            pltpu.VMEM((4, 16, 256), F32),
            pltpu.VMEM((8, 27, 128, 128), F32),
            pltpu.SemaphoreType.DMA((4,)),
            pltpu.SemaphoreType.DMA((27,)),
            pltpu.SemaphoreType.DMA((27,)),
            pltpu.SemaphoreType.DMA((27,)),
            pltpu.SemaphoreType.DMA((27,)),
        ],
        compiler_params=pltpu.CompilerParams(
            collective_id=0, has_side_effects=True, vmem_limit_bytes=56 * 2**20
        ),
        name="sph",
    )(offsets, velocity, mass, counts)


def solution(mesh):
    sizes = tuple(mesh.shape[a] for a in AXES)
    in_specs = (
        P(None, "gx", "gy", "gz", None),
        P(None, "gx", "gy", "gz", None),
        P("gx", "gy", "gz", None),
        P("gx", "gy", "gz"),
    )
    out_specs = (P(None, "gx", "gy", "gz", None), P("gx", "gy", "gz", None))
    return jax.shard_map(
        functools.partial(local, sizes), mesh=mesh, in_specs=in_specs, out_specs=out_specs, check_vma=False
    )
```

time: 54.5 us -> 49.7 us (0.912)
  Pallas kernels: 49.5 us -> 46.9 us
  local copies, waits for them, and re-layouts: 3.97 us -> 1.9 us
    pallas_call x1, Pallas kernels: 49.5 us -> 46.9 us  [local(): pl.pallas_call(functools.partial(kernel, sizes), out_shape=(jax.ShapeDtyp...]
    unnamed x10 -> x4, local copies, waits for them, and re-layouts: 3.97 us -> 1.9 us
where the time goes in v1:
time: 49.7 us; the launch traced here: 49.5 us
  Pallas kernels  46.9 us (94%)
  local copies, waits for them, and re-layouts  1.9 us (4%)
  between operations  0.65 us (1%)
    pallas_call x1, Pallas kernels, local(): pl.pallas_call(functools.partial(kernel, sizes), out_shape=(jax.ShapeDtyp...  46.9 us
    unnamed x4, local copies, waits for them, and re-layouts  1.9 us

profile of v1, /device:TPU:71, one launch (start us, length us, event | category | flops | bytes accessed | tf_op | source)
XLA Modules:
  0.0 49.5 jit_solution(15620038925048000089)
XLA Ops:
  0.6 46.9 %sph.1 = (f32[3,2,2,2,128]{4,3,2,1,0:T(2,128)}, f32[2,2,2,128]{3,2,1,0:T(2,128)}) custom-call(f32[3,2,2,2,128]{4,3,2,1,0:T(2,128)} %off_in.1, f32[3,2,2,2,128]{4,3,2,1,0:T(2,128)} %vel_in.1, f32[2,2,2,128]{3,2,1,0:T(2,128)} %mass_in.1, s32[2,2,2]{2,1,0:T(2,128)} %cnt_in.1), custom_call_target="tpu_custom_call" | custom-call | tf_op jit(solution)/shard_map/sph/pallas_call | solution.py:370
  47.5 0.0 copy-start
  47.6 1.3 %copy.8 = f32[3,2,2,2,128]{4,3,2,1,0:T(2,128)} copy(f32[3,2,2,2,128]{4,3,2,1,0:T(2,128)} %get-tuple-element.4) | data formatting | bytes 24576
  48.9 0.0 copy-done
  48.9 0.6 %copy.9 = f32[2,2,2,128]{3,2,1,0:T(2,128)} copy(f32[2,2,2,128]{3,2,1,0:T(2,128)S(1)} %copy-done) | data formatting | bytes 8192
Async XLA Ops:
  47.5 1.3 %copy-start = (f32[2,2,2,128]{3,2,1,0:T(2,128)S(1)}, f32[2,2,2,128]{3,2,1,0:T(2,128)}, u32[]{:S(2)}) copy-start(f32[2,2,2,128]{3,2,1,0:T(2,128)} %get-tuple-element.5) | copy-start | bytes 12292

commit v2 on v1

--- a/solution.py
+++ b/solution.py
@@ -18,7 +18,10 @@
 BF16 = jnp.bfloat16
 TILE = 32
 LAST = (((1,), (1,)), ((), ()))
-SHARED = (6, 4, 6)
+SHARED = (4, 4, 4, 2)
+WHOLE = (8, 10, 6, 3)
+SHARED_BASE = tuple(sum(SHARED[:k]) for k in range(5))
+REST_BASE = tuple(sum(WHOLE[:k]) - sum(SHARED[:k]) for k in range(5))
 
 
 def span_own(step):
@@ -49,8 +52,8 @@
     return high, (x - high.astype(F32)).astype(BF16)
 
 
-def kernel(sizes, off_in, vel_in, mass_in, cnt_in, acc_out, den_out, off, vel, mass, cnt, own, near, u_own, u_near,
-           own_q, near_q, near_f, s_b, dens, force, force2, force3, quad, load, send1, recv1, send2, recv2):
+def kernel(sizes, off_in, vel_in, mass_in, cnt_in, acc_out, den_out, off, vel, mass, cnt, own, near, s_own, u_own, u_near,
+           own_q, near_q, near_f, s_b, dens, force, force2, force3, quad, split, load, send1, recv1, send2, recv2):
     me = tuple(lax.axis_index(a) for a in AXES)
     near_x = 1 - 2 * lax.rem(me[0], 2)
     far_x = -near_x
@@ -160,11 +163,14 @@
         shared = [(a, bh, c) for a in (1, 2) for c in (1, 2)]
         return shared + [(a, b, ch) for a in (1, 2) for b in (bh, 1, 2)]
 
-    def cells_side(x, y, z):
-        shared = [(3 * x, y + b, c) for b in range(3) for c in (1, 2)]
-        return shared + [(3 * x, y + b, 3 * z) for b in range(3)]
-
-    def density_cells(x, cells_of, base, first):
+    def cells_inner(x, y, z):
+        return [(3 * x, b, c) for b in (1, 2) for c in (1, 2)] + [(3 * x, b, 3 * z) for b in (1, 2)]
+
+    def cells_outer(x, y, z):
+        return [(3 * x, 3 * y, c) for c in (1, 2, 3 * z)]
+
+    def density_cells(x, cells_of, stage, first):
+        shared = SHARED[stage]
         for y in range(2):
             for z in range(2):
                 n = 4 * x + 2 * y + z
@@ -177,46 +183,68 @@
                     both = jnp.dot(mine, them, preferred_element_type=F32)
                     for i, (a, b, c) in enumerate(group):
                         q = jnp.maximum(both[:, 128 * i : 128 * i + 128], 0.0)
-                        quad[n, base + k + i] = q
-                        total = total + (q * q) * (q * near[a, b, c, 3:4, :])
+                        q2 = q * q
+                        q3 = q2 * q
+                        if k < shared:
+                            place = (n, SHARED_BASE[stage] + k + i)
+                            for p, part in enumerate(halves(q2) + halves(q3)):
+                                split[(p,) + place] = part
+                        else:
+                            quad[n, REST_BASE[stage] + k + i - shared] = q
+                        total = total + q3 * near[a, b, c, 3:4, :]
                 dens[n] = total
 
-    def force_pair(x, y, cells_of, base, shared, first):
+    def force_pair(x, y, cells_of, stage, first):
         n = 4 * x + 2 * y
         pair = 2 * x + y
-        rows2 = jnp.zeros((32, 256), F32) if first else force2[pair]
-        rows3 = jnp.zeros((16, 256), F32) if first else force3[pair]
+        shared = SHARED[stage]
         cells = cells_of(x, y, 0)
-        for k in range(0, shared, 2):
+        grams = [
+            jnp.zeros((32, 256), F32) if first else force2[pair],
+            jnp.zeros((16, 256), F32) if first else force3[pair],
+        ]
+
+        def gram(k):
             f = jnp.concatenate([near_f[cells[k]], near_f[cells[k + 1]]], axis=1)
-            q = jnp.concatenate(
-                [jnp.concatenate([quad[n + z, base + k + i] for i in range(2)], axis=1) for z in range(2)], axis=0
-            )
-            q2 = q * q
-            for part in halves(q2):
-                rows2 = rows2 + lax.dot_general(f[:32], part, LAST, preferred_element_type=F32)
-            for part in halves(q2 * q):
-                rows3 = rows3 + lax.dot_general(f[32:], part, LAST, preferred_element_type=F32)
-        force2[pair] = rows2
-        force3[pair] = rows3
-        for z in range(2):
-            rest = list(enumerate(cells_of(x, y, z)))[shared:]
-            for r0 in range(0, 128, TILE):
-                rows = pl.ds(r0, TILE)
-                si = s_b[n + z, rows, :]
-                sums = [jnp.zeros((TILE, 128), F32) if first else force[k, n + z, rows, :] for k in range(5)]
-                for k, (a, b, c) in rest:
-                    t = near[a, b, c]
-                    q = quad[n + z, base + k, rows, :]
-                    q2 = q * q
-                    pr = q2 * (t[3:4] * si + t[7:8])
-                    vi = q2 * (q * t[7:8])
-                    for d in range(3):
-                        sums[d] = sums[d] + (pr * t[d : d + 1] + vi * t[4 + d : 5 + d])
-                    sums[3] = sums[3] + pr
-                    sums[4] = sums[4] + vi
-                for k in range(5):
-                    force[k, n + z, rows, :] = sums[k]
+            for p in range(4):
+                place = SHARED_BASE[stage] + k
+                part = jnp.concatenate(
+                    [jnp.concatenate([split[p, n + z, place + i] for i in range(2)], axis=1) for z in range(2)], axis=0
+                )
+                rows = f[:32] if p < 2 else f[32:]
+                grams[p // 2] = grams[p // 2] + lax.dot_general(rows, part, LAST, preferred_element_type=F32)
+
+        def direct(z, r0):
+            rest = cells_of(x, y, z)[shared:]
+            rows = pl.ds(r0, TILE)
+            si = s_b[n + z, rows, :]
+            sums = [jnp.zeros((TILE, 128), F32) if first else force[k, n + z, rows, :] for k in range(5)]
+            for k, (a, b, c) in enumerate(rest):
+                t = near[a, b, c]
+                q = quad[n + z, REST_BASE[stage] + k, rows, :]
+                q2 = q * q
+                pr = q2 * (t[3:4] * si + t[7:8])
+                vi = q2 * (q * t[7:8])
+                for d in range(3):
+                    sums[d] = sums[d] + (pr * t[d : d + 1] + vi * t[4 + d : 5 + d])
+                sums[3] = sums[3] + pr
+                sums[4] = sums[4] + vi
+            for k in range(5):
+                force[k, n + z, rows, :] = sums[k]
+
+        tiles = [(z, r0) for z in range(2) for r0 in range(0, 128, TILE)]
+        steps = shared // 2
+        done = 0
+        for k in range(steps):
+            gram(2 * k)
+            until = len(tiles) * (k + 1) // steps
+            for z, r0 in tiles[done:until]:
+                direct(z, r0)
+            done = until
+        for z, r0 in tiles[done:]:
+            direct(z, r0)
+        force2[pair] = grams[0]
+        force3[pair] = grams[1]
 
     def over_x(fn):
         def step(x, carry):
@@ -225,9 +253,9 @@
 
         lax.fori_loop(0, 2, step, 0)
 
-    def force_cells(x, cells_of, base, shared, first):
+    def force_cells(x, cells_of, stage, first):
         for y in range(2):
-            force_pair(x, y, cells_of, base, shared, first)
+            force_pair(x, y, cells_of, stage, first)
 
     def corner(step):
         def low(s):
@@ -297,65 +325,86 @@
                     for cell in cells:
                         near_f[cell] = jnp.zeros((48, 128), BF16)
 
+    def densities(x):
+        four = [(y, z) for y in range(2) for z in range(2)]
+        rows = []
+        for y, z in four:
+            rho = KERNEL_NORM * jnp.sum(jnp.transpose(dens[4 * x + 2 * y + z], (1, 0)), axis=0, keepdims=True)
+            held = lanes < cnt[x, y, z]
+            rho = jnp.where(held, rho, 0.0)
+            den_out[x, y, z : z + 1, :] = rho
+            s = PRESSURE_COEF / jnp.where(held, rho, 1.0)
+            rows.append(s)
+            s_own[x, y, z] = s
+            u_own[x, y, z] = own[x, y, z, 3:4, :] * s
+        return rows
+
+    def prepare(x, rows):
+        turned = jnp.transpose(jnp.concatenate(rows + rows, axis=0), (1, 0))
+        for k in range(4):
+            y, z = k // 2, k % 2
+            s_b[4 * x + k] = jnp.broadcast_to(turned[:, k : k + 1], (128, 128))
+            u = own[x, y, z, 3:4, :] * rows[k]
+            near[1 + x, 1 + y, 1 + z, 7:8, :] = u
+            put_near_f(1 + x, 1 + y, 1 + z, u)
+
+    def post2(dirs):
+        for step in dirs:
+            @pl.when(exists(step))
+            def _():
+                copy2(step, False).start()
+
+    def finish(x):
+        for y in range(2):
+            for z in range(2):
+                n, pair = 4 * x + 2 * y + z, 2 * x + y
+                f = [jnp.sum(jnp.transpose(force[k, n], (1, 0)), axis=0, keepdims=True) for k in range(5)]
+                g = force2[pair, :, 128 * z : 128 * z + 128]
+                g = g[0:8] + g[8:16] + g[16:24]
+                h = force3[pair, :, 128 * z : 128 * z + 128]
+                h = h[0:4] + h[4:8] + h[8:12]
+                held = lanes < cnt[x, y, z]
+                t = own[x, y, z]
+                s = s_own[x, y, z]
+                press = f[3] + s * g[0:1] + g[4:5]
+                drag = f[4] + h[0:1]
+                for k in range(3):
+                    a = f[k] + s * g[1 + k : 2 + k] + g[5 + k : 6 + k] + h[1 + k : 2 + k]
+                    a = KERNEL_NORM * (a + GRADIENT_RATIO * t[k : k + 1] * press - t[4 + k : 5 + k] * drag)
+                    acc_out[k, x, y, z : z + 1, :] = jnp.where(held, a, 0.0)
+
     near_side, far_side = (near_x + 1) // 2, (far_x + 1) // 2
+    far_inner, far_outer = [d for d in far_dirs if d[1] == 0], [d for d in far_dirs if d[1] != 0]
     over_x(lambda x: density_cells(x, cells_own, 0, True))
     arrive1(plane_dirs)
-    over_x(lambda x: density_cells(x, cells_plane, 8, False))
+    over_x(lambda x: density_cells(x, cells_plane, 1, False))
     arrive1(near_dirs)
-    density_cells(near_side, cells_side, 18, False)
-    arrive1(far_dirs)
-    density_cells(far_side, cells_side, 18, False)
-
-    s_rows = []
-    for n in range(8):
-        x, y, z = n // 4, (n // 2) % 2, n % 2
-        rho = KERNEL_NORM * jnp.sum(jnp.transpose(dens[n], (1, 0)), axis=0, keepdims=True)
-        held = lanes < cnt[x, y, z]
-        rho = jnp.where(held, rho, 0.0)
-        den_out[x, y, z : z + 1, :] = rho
-        s = PRESSURE_COEF / jnp.where(held, rho, 1.0)
-        s_rows.append(s)
-        u = own[x, y, z, 3:4, :] * s
-        u_own[x, y, z] = u
-
-    for step in all_dirs:
-        @pl.when(exists(step))
-        def _():
-            copy2(step, False).start()
-
-    s_all = jnp.concatenate(s_rows, axis=0)
-    turned = jnp.transpose(s_all, (1, 0))
-    for n in range(8):
-        x, y, z = n // 4, (n // 2) % 2, n % 2
-        s_b[n] = jnp.broadcast_to(turned[:, n : n + 1], (128, 128))
-        u = own[x, y, z, 3:4, :] * s_rows[n]
-        near[1 + x, 1 + y, 1 + z, 7:8, :] = u
-        put_near_f(1 + x, 1 + y, 1 + z, u)
-
-    over_x(lambda x: force_cells(x, cells_own, 0, SHARED[0], True))
+    density_cells(near_side, cells_inner, 2, False)
+    density_cells(near_side, cells_outer, 3, False)
+    rows = densities(near_side)
+    post2(near_dirs)
+    prepare(near_side, rows)
+    arrive1(far_inner)
+    density_cells(far_side, cells_inner, 2, False)
+    arrive1(far_outer)
+    density_cells(far_side, cells_outer, 3, False)
+    rows = densities(far_side)
+    post2(far_dirs)
+    post2(plane_dirs)
+    prepare(far_side, rows)
+
+    over_x(lambda x: force_cells(x, cells_own, 0, True))
     arrive2(plane_dirs)
-    over_x(lambda x: force_cells(x, cells_plane, 8, SHARED[1], False))
+    over_x(lambda x: force_cells(x, cells_plane, 1, False))
     arrive2(near_dirs)
-    force_cells(near_side, cells_side, 18, SHARED[2], False)
-    arrive2(far_dirs)
-    force_cells(far_side, cells_side, 18, SHARED[2], False)
-
-    for n in range(8):
-        x, y, z = n // 4, (n // 2) % 2, n % 2
-        f = [jnp.sum(jnp.transpose(force[k, n], (1, 0)), axis=0, keepdims=True) for k in range(5)]
-        g = force2[2 * x + y, :, 128 * z : 128 * z + 128]
-        g = g[0:8] + g[8:16] + g[16:24]
-        h = force3[2 * x + y, :, 128 * z : 128 * z + 128]
-        h = h[0:4] + h[4:8] + h[8:12]
-        held = lanes < cnt[x, y, z]
-        t = own[x, y, z]
-        s = s_rows[n]
-        press = f[3] + s * g[0:1] + g[4:5]
-        drag = f[4] + h[0:1]
-        for k in range(3):
-            a = f[k] + s * g[1 + k : 2 + k] + g[5 + k : 6 + k] + h[1 + k : 2 + k]
-            a = KERNEL_NORM * (a + GRADIENT_RATIO * t[k : k + 1] * press - t[4 + k : 5 + k] * drag)
-            acc_out[k, x, y, z : z + 1, :] = jnp.where(held, a, 0.0)
+    force_cells(near_side, cells_inner, 2, False)
+    force_cells(near_side, cells_outer, 3, False)
+    finish(near_side)
+    arrive2(far_inner)
+    force_cells(far_side, cells_inner, 2, False)
+    arrive2(far_outer)
+    force_cells(far_side, cells_outer, 3, False)
+    finish(far_side)
 
     for step in all_dirs:
         @pl.when(exists(step))
@@ -370,8 +419,8 @@
     return pl.pallas_call(
         functools.partial(kernel, sizes),
         out_shape=(
-            jax.ShapeDtypeStruct(offsets.shape, F32),
-            jax.ShapeDtypeStruct(mass.shape, F32),
+            pltpu.VMEM(offsets.shape, F32),
+            pltpu.VMEM(mass.shape, F32),
         ),
         in_specs=[hbm, hbm, hbm, hbm],
         out_specs=(vmem, vmem),
@@ -383,6 +432,7 @@
             pltpu.VMEM((2, 2, 2, 8, 128), F32),
             pltpu.VMEM((4, 4, 4, 8, 128), F32),
             pltpu.VMEM((2, 2, 2, 1, 128), F32),
+            pltpu.VMEM((2, 2, 2, 1, 128), F32),
             pltpu.VMEM((4, 4, 4, 1, 128), F32),
             pltpu.VMEM((8, 128, 48), BF16),
             pltpu.VMEM((4, 4, 4, 48, 128), BF16),
@@ -392,7 +442,8 @@
             pltpu.VMEM((5, 8, 128, 128), F32),
             pltpu.VMEM((4, 32, 256), F32),
             pltpu.VMEM((4, 16, 256), F32),
-            pltpu.VMEM((8, 27, 128, 128), F32),
+            pltpu.VMEM((8, REST_BASE[4], 128, 128), F32),
+            pltpu.VMEM((4, 8, SHARED_BASE[4], 128, 128), BF16),
             pltpu.SemaphoreType.DMA((4,)),
             pltpu.SemaphoreType.DMA((27,)),
             pltpu.SemaphoreType.DMA((27,)),

time: 49.7 us -> 48.3 us (0.972)
  local copies, waits for them, and re-layouts: 1.9 us -> 1.19 us
  Pallas kernels: 46.9 us -> 46.3 us
    unnamed x4 -> x2, local copies, waits for them, and re-layouts: 1.9 us -> 1.19 us
    pallas_call x1, Pallas kernels: 46.9 us -> 46.3 us  [local(): pl.pallas_call(functools.partial(kernel, sizes), out_shape=(pltpu.VMEM(of...]
where the time goes in v2:
time: 48.3 us; the launch traced here: 48.1 us
  Pallas kernels  46.3 us (96%)
  local copies, waits for them, and re-layouts  1.19 us (2%)
  between operations  0.64 us (1%)
    pallas_call x1, Pallas kernels, local(): pl.pallas_call(functools.partial(kernel, sizes), out_shape=(pltpu.VMEM(of...  46.3 us
    unnamed x2, local copies, waits for them, and re-layouts  1.19 us

profile of v2, /device:TPU:71, one launch (start us, length us, event | category | flops | bytes accessed | tf_op | source)
XLA Modules:
  0.0 48.1 jit_solution(5568161499578273754)
XLA Ops:
  0.6 46.3 %sph.1 = (f32[3,2,2,2,128]{4,3,2,1,0:T(2,128)S(1)}, f32[2,2,2,128]{3,2,1,0:T(2,128)S(1)}) custom-call(f32[3,2,2,2,128]{4,3,2,1,0:T(2,128)} %off_in.1, f32[3,2,2,2,128]{4,3,2,1,0:T(2,128)} %vel_in.1, f32[2,2,2,128]{3,2,1,0:T(2,128)} %mass_in.1, s32[2,2,2]{2,1,0:T(2,128)} %cnt_in.1), custom_call_target="tpu_custom_call" | custom-call | tf_op jit(solution)/shard_map/sph/pallas_call | solution.py:419
  46.9 0.6 %copy.8 = f32[3,2,2,2,128]{4,3,2,1,0:T(2,128)} copy(f32[3,2,2,2,128]{4,3,2,1,0:T(2,128)S(1)} %get-tuple-element.2) | data formatting | bytes 24576
  47.5 0.6 %copy.9 = f32[2,2,2,128]{3,2,1,0:T(2,128)} copy(f32[2,2,2,128]{3,2,1,0:T(2,128)S(1)} %get-tuple-element.3) | data formatting | bytes 8192

commit v3 on v2

--- a/solution.py
+++ b/solution.py
@@ -53,14 +53,15 @@
 
 
 def kernel(sizes, off_in, vel_in, mass_in, cnt_in, acc_out, den_out, off, vel, mass, cnt, own, near, s_own, u_own, u_near,
-           own_q, near_q, near_f, s_b, dens, force, force2, force3, quad, split, load, send1, recv1, send2, recv2):
+           own_q, near_q, near_f, s_b, dens, force, force2, force3, quad, split, load, send1, recv1, send2, recv2, send3, recv3):
     me = tuple(lax.axis_index(a) for a in AXES)
     near_x = 1 - 2 * lax.rem(me[0], 2)
     far_x = -near_x
     plane_dirs = [(0, b, c) for b in SIDES for c in SIDES if (b, c) != (0, 0)]
     near_dirs = [(near_x, b, c) for b in SIDES for c in SIDES]
     far_dirs = [(far_x, b, c) for b in SIDES for c in SIDES]
-    all_dirs = far_dirs + near_dirs + plane_dirs
+    far_inner, far_outer = [d for d in far_dirs if d[1] == 0], [d for d in far_dirs if d[1] != 0]
+    all_dirs = far_outer + far_inner + near_dirs + plane_dirs
 
     def other(step):
         return tuple(m + s for m, s in zip(me, step))
@@ -81,14 +82,14 @@
         pltpu.make_async_copy(src, dst, load.at[k])
         for k, (src, dst) in enumerate(((off_in, off), (mass_in, mass), (cnt_in, cnt), (vel_in, vel)))
     ]
-    for item in loads:
-        item.start()
     barrier = pltpu.get_barrier_semaphore()
     for step in all_dirs:
         @pl.when(exists(step))
         def _():
             pl.semaphore_signal(barrier, inc=1, device_id=other(step), device_id_type=MESH)
     for item in loads:
+        item.start()
+    for item in loads:
         item.wait()
 
     lanes = lax.broadcasted_iota(jnp.int32, (1, 128), 1)
@@ -117,13 +118,15 @@
         peers = peers * (1 + (m > 0).astype(jnp.int32) + (m < n - 1).astype(jnp.int32))
     pl.semaphore_wait(barrier, peers - 1)
 
-    def copy1(step, incoming):
+    def copy1(step, incoming, half=0):
         there = step if incoming else neg(step)
+        rows = (pl.ds(4 * half, 4),)
+        send, recv = ((send1, recv1), (send3, recv3))[half]
         return pltpu.make_async_remote_copy(
-            src_ref=own.at[tuple(span_own(s) for s in step)],
-            dst_ref=near.at[tuple(span_halo(s) for s in there)],
-            send_sem=send1.at[slot(step)],
-            recv_sem=recv1.at[slot(there)],
+            src_ref=own.at[tuple(span_own(s) for s in step) + rows],
+            dst_ref=near.at[tuple(span_halo(s) for s in there) + rows],
+            send_sem=send.at[slot(step)],
+            recv_sem=recv.at[slot(there)],
             device_id=other(step),
             device_id_type=MESH,
         )
@@ -143,6 +146,11 @@
         @pl.when(exists(step))
         def _():
             copy1(step, False).start()
+
+    for step in all_dirs:
+        @pl.when(exists(step))
+        def _():
+            copy1(step, False, 1).start()
 
     for x in range(2):
         for y in range(2):
@@ -271,29 +279,31 @@
             for k in range(many(step[2]))
         ]
 
+    def clear(dirs):
+        for step in dirs:
+            @pl.when(jnp.logical_not(exists(step)))
+            def _():
+                for cell in corner(step):
+                    near[cell] = jnp.zeros((8, 128), F32)
+                    u_near[cell] = jnp.zeros((1, 128), F32)
+
     def arrive1(dirs):
         for step in dirs:
-            cells = corner(step)
-
             @pl.when(exists(step))
             def _():
                 copy1(step, True).wait_recv()
-                for a, b, c in cells:
-                    t = near[a, b, c]
-                    pos = []
-                    for k in range(3):
-                        shift = 2 * step[k]
-                        pos.append(t[k : k + 1] + (float(shift) if isinstance(shift, int) else shift.astype(F32)))
-                    sq = pos[0] * pos[0] + pos[1] * pos[1] + pos[2] * pos[2]
-                    scaled = [p * -6.0 for p in pos]
-                    near[a, b, c, 0:3, :] = jnp.concatenate(scaled, axis=0)
-                    put_near_q(a, b, c, scaled, 1.0 - sq)
-
-            @pl.when(jnp.logical_not(exists(step)))
-            def _():
-                for cell in cells:
-                    near[cell] = jnp.zeros((8, 128), F32)
-                    near_q[cell] = jnp.zeros((48, 128), BF16)
+
+        for step in dirs:
+            for a, b, c in corner(step):
+                t = near[a, b, c, 0:4, :]
+                pos = []
+                for k in range(3):
+                    shift = 2 * step[k]
+                    pos.append(t[k : k + 1] + (float(shift) if isinstance(shift, int) else shift.astype(F32)))
+                sq = pos[0] * pos[0] + pos[1] * pos[1] + pos[2] * pos[2]
+                scaled = [p * -6.0 for p in pos]
+                near[a, b, c, 0:3, :] = jnp.concatenate(scaled, axis=0)
+                put_near_q(a, b, c, scaled, 1.0 - sq)
 
     def put_near_f(a, b, c, u):
         t = near[a, b, c]
@@ -307,23 +317,18 @@
 
     def arrive2(dirs):
         for step in dirs:
-            cells = corner(step)
-            inner = isinstance(step[2], int) and step[2] == 0
-
             @pl.when(exists(step))
             def _():
+                copy1(step, True, 1).wait_recv()
                 copy2(step, True).wait_recv()
-                for a, b, c in cells:
-                    u = u_near[a, b, c]
-                    near[a, b, c, 7:8, :] = u
-                    if inner:
-                        put_near_f(a, b, c, u)
-
-            if inner:
-                @pl.when(jnp.logical_not(exists(step)))
-                def _():
-                    for cell in cells:
-                        near_f[cell] = jnp.zeros((48, 128), BF16)
+
+        for step in dirs:
+            inner = isinstance(step[2], int) and step[2] == 0
+            for a, b, c in corner(step):
+                u = u_near[a, b, c]
+                near[a, b, c, 7:8, :] = u
+                if inner:
+                    put_near_f(a, b, c, u)
 
     def densities(x):
         four = [(y, z) for y in range(2) for z in range(2)]
@@ -374,7 +379,7 @@
                     acc_out[k, x, y, z : z + 1, :] = jnp.where(held, a, 0.0)
 
     near_side, far_side = (near_x + 1) // 2, (far_x + 1) // 2
-    far_inner, far_outer = [d for d in far_dirs if d[1] == 0], [d for d in far_dirs if d[1] != 0]
+    clear(all_dirs)
     over_x(lambda x: density_cells(x, cells_own, 0, True))
     arrive1(plane_dirs)
     over_x(lambda x: density_cells(x, cells_plane, 1, False))
@@ -389,7 +394,8 @@
     arrive1(far_outer)
     density_cells(far_side, cells_outer, 3, False)
     rows = densities(far_side)
-    post2(far_dirs)
+    post2(far_outer)
+    post2(far_inner)
     post2(plane_dirs)
     prepare(far_side, rows)
 
@@ -410,6 +416,7 @@
         @pl.when(exists(step))
         def _():
             copy1(step, False).wait_send()
+            copy1(step, False, 1).wait_send()
             copy2(step, False).wait_send()
 
 
@@ -449,6 +456,8 @@
             pltpu.SemaphoreType.DMA((27,)),
             pltpu.SemaphoreType.DMA((27,)),
             pltpu.SemaphoreType.DMA((27,)),
+            pltpu.SemaphoreType.DMA((27,)),
+            pltpu.SemaphoreType.DMA((27,)),
         ],
         compiler_params=pltpu.CompilerParams(
             collective_id=0, has_side_effects=True, vmem_limit_bytes=56 * 2**20

time: 48.3 us -> 48.4 us (level)
  the two profiles are of different devices: /device:TPU:71 before, /device:TPU:39 now
where the time goes in v3:
time: 48.4 us; the launch traced here: 48.2 us
  Pallas kernels  46.4 us (96%)
  local copies, waits for them, and re-layouts  1.19 us (2%)
  between operations  0.64 us (1%)
    pallas_call x1, Pallas kernels, local(): pl.pallas_call(functools.partial(kernel, sizes), out_shape=(pltpu.VMEM(of...  46.4 us
    unnamed x2, local copies, waits for them, and re-layouts  1.19 us

profile of v3, /device:TPU:39, one launch (start us, length us, event | category | flops | bytes accessed | tf_op | source)
XLA Modules:
  0.0 48.2 jit_solution(9926333287794372754)
XLA Ops:
  0.6 46.4 %sph.1 = (f32[3,2,2,2,128]{4,3,2,1,0:T(2,128)S(1)}, f32[2,2,2,128]{3,2,1,0:T(2,128)S(1)}) custom-call(f32[3,2,2,2,128]{4,3,2,1,0:T(2,128)} %off_in.1, f32[3,2,2,2,128]{4,3,2,1,0:T(2,128)} %vel_in.1, f32[2,2,2,128]{3,2,1,0:T(2,128)} %mass_in.1, s32[2,2,2]{2,1,0:T(2,128)} %cnt_in.1), custom_call_target="tpu_custom_call" | custom-call | tf_op jit(solution)/shard_map/sph/pallas_call | solution.py:426
  47.0 0.6 %copy.8 = f32[3,2,2,2,128]{4,3,2,1,0:T(2,128)} copy(f32[3,2,2,2,128]{4,3,2,1,0:T(2,128)S(1)} %get-tuple-element.2) | data formatting | bytes 24576
  47.6 0.6 %copy.9 = f32[2,2,2,128]{3,2,1,0:T(2,128)} copy(f32[2,2,2,128]{3,2,1,0:T(2,128)S(1)} %get-tuple-element.3) | data formatting | bytes 8192
